TPU v7x, 32 devices: a whole 2x2x4 slice. The times are simulated.
32 devices in a mesh: dp: 8 (over y, x, core), tensor: 4 (over z).
Axes of the slice: x: 2, y: 2, z: 4, core: 2. Of those that a mesh axis runs over, the one named last changes fastest.
Arguments:
- tokens: bfloat16 [8, 584, 1024], P('dp', 'tensor'), may hold values from -6 to 6
- cotangent: bfloat16 [8, 584, 1024], P('dp', 'tensor'), may hold values from -6 to 6
- image_mask: int32 [8], P('dp'), may hold values 0 or 1
- qkv_weight: bfloat16 [2, 1024, 3, 1024], P(None, 'dp', None, 'tensor'), may hold values from -0.1875 to 0.1875
- out_weight: bfloat16 [2, 1024, 1024], P(None, 'dp', 'tensor'), may hold values from -2 to 2
- up_weight: bfloat16 [2, 1024, 4096], P(None, 'dp', 'tensor'), may hold values from -0.1875 to 0.1875
- down_weight: bfloat16 [2, 1024, 4096], P(None, 'dp', 'tensor'), may hold values from -0.09375 to 0.09375
- qv_bias: bfloat16 [2, 2, 1024], P(None, None, ('dp', 'tensor')), may hold values from -3 to 3
- up_bias: bfloat16 [2, 4096], P(None, ('dp', 'tensor')), may hold values from -3 to 3
- out_bias: bfloat16 [2, 1024], P(None, ('dp', 'tensor')), may hold values from -3 to 3
- down_bias: bfloat16 [2, 1024], P(None, ('dp', 'tensor')), may hold values from -3 to 3
- attn_gain: bfloat16 [2, 1024], P(None, ('dp', 'tensor')), may hold values from 0.5 to 1.5
- attn_shift: bfloat16 [2, 1024], P(None, ('dp', 'tensor')), may hold values from -3 to 3
- mlp_gain: bfloat16 [2, 1024], P(None, ('dp', 'tensor')), may hold values from 0.5 to 1.5
- mlp_shift: bfloat16 [2, 1024], P(None, ('dp', 'tensor')), may hold values from -3 to 3
Outputs:
- output: bfloat16 [8, 584, 1024], P('dp', 'tensor')
- input_grad: float32 [8, 584, 1024], P('dp', 'tensor')
- qkv_weight_grad: float32 [2, 1024, 3, 1024], P(None, 'dp', None, 'tensor')
- out_weight_grad: float32 [2, 1024, 1024], P(None, 'dp', 'tensor')
- up_weight_grad: float32 [2, 1024, 4096], P(None, 'dp', 'tensor')
- down_weight_grad: float32 [2, 1024, 4096], P(None, 'dp', 'tensor')
- qv_bias_grad: float32 [2, 2, 1024], P(None, None, ('dp', 'tensor'))
- up_bias_grad: float32 [2, 4096], P(None, ('dp', 'tensor'))
- out_bias_grad: float32 [2, 1024], P(None, ('dp', 'tensor'))
- down_bias_grad: float32 [2, 1024], P(None, ('dp', 'tensor'))
- attn_gain_grad: float32 [2, 1024], P(None, ('dp', 'tensor'))
- attn_shift_grad: float32 [2, 1024], P(None, ('dp', 'tensor'))
- mlp_gain_grad: float32 [2, 1024], P(None, ('dp', 'tensor'))
- mlp_shift_grad: float32 [2, 1024], P(None, ('dp', 'tensor'))
All inputs are finite; a program needn't handle non-finite values. No bound on the sum of `image_mask` on one device may be relied on, other than what follows from the above.
Results may differ from a plain program's by a relative error of at most 0.017.
Values may be sent and summed in bfloat16 or wider, within the bound.
A program may use at most 192 MiB of HBM per device.

v0:
```python
import math

import jax
import jax.numpy as jnp
from jax import lax
from jax.sharding import PartitionSpec as P

HD = 64
VALID = 577


norm_eps = 1e-06
root_half = 0.7071067811865476
far_below = -1e30


def layer_norm(values, gain_vec, shift_vec):
    centre = values - jnp.mean(values, axis=-1, keepdims=True)
    spread = jnp.mean(centre * centre, axis=-1, keepdims=True)
    return centre * lax.rsqrt(spread + norm_eps) * gain_vec + shift_vec


def gelu_exact(values):
    return 0.5 * values * (1.0 + lax.erf(values * root_half))


def spread_rows(normed):
    return lax.all_gather(normed, "tensor", axis=1, tiled=True)


def gather_grads(grad_low):
    return lax.all_gather(grad_low, "tensor", axis=1, tiled=True)


def branch_total(partial_rows):
    return lax.psum_scatter(
        partial_rows.astype(jnp.bfloat16), "tensor", scatter_dimension=1, tiled=True
    ).astype(jnp.float32)


def grad_total(partial_rows):
    return lax.psum_scatter(
        partial_rows.astype(jnp.bfloat16), "tensor", scatter_dimension=1, tiled=True
    ).astype(jnp.float32)


def masked_scores(q_heads, k_heads, key_valid, score_scale):
    raw_scores = (
        jnp.einsum("qhd,khd->hqk", q_heads, k_heads, preferred_element_type=jnp.float32)
        * score_scale
    )
    return jnp.where(key_valid[None, None, :], raw_scores, far_below)


def attend_image(block_in, key_valid, head_size):
    queries, key_rows, value_rows = block_in
    seq_len = queries.shape[0]
    score_scale = 1.0 / math.sqrt(head_size)
    q_heads = queries.reshape(seq_len, -1, head_size)
    k_heads = key_rows.reshape(seq_len, -1, head_size)
    v_heads = value_rows.reshape(seq_len, -1, head_size)
    scores = masked_scores(q_heads, k_heads, key_valid, score_scale)
    row_top = jnp.max(scores, axis=-1, keepdims=True)
    weights = jnp.exp(scores - row_top)
    totals = jnp.sum(weights, axis=-1, keepdims=True)
    probabilities = (weights / totals).astype(jnp.bfloat16)
    mixed_rows = jnp.einsum(
        "hqk,khd->qhd", probabilities, v_heads, preferred_element_type=jnp.float32
    )
    log_total = (row_top + jnp.log(totals))[..., 0]
    return (mixed_rows.reshape(seq_len, -1).astype(jnp.bfloat16), log_total)


def attend_back_image(block_in, key_valid, head_size):
    queries, key_rows, value_rows, log_total, mixed_grad = block_in
    seq_len = queries.shape[0]
    score_scale = 1.0 / math.sqrt(head_size)
    q_heads = queries.reshape(seq_len, -1, head_size)
    k_heads = key_rows.reshape(seq_len, -1, head_size)
    v_heads = value_rows.reshape(seq_len, -1, head_size)
    g_heads = mixed_grad.reshape(seq_len, -1, head_size)
    scores = masked_scores(q_heads, k_heads, key_valid, score_scale)
    probabilities = jnp.exp(scores - log_total[..., None])
    value_grad = jnp.einsum(
        "hqk,qhd->khd",
        probabilities.astype(jnp.bfloat16),
        g_heads,
        preferred_element_type=jnp.float32,
    )
    prob_grad = jnp.einsum("qhd,khd->hqk", g_heads, v_heads, preferred_element_type=jnp.float32)
    row_inner = jnp.sum(prob_grad * probabilities, axis=-1, keepdims=True)
    score_grad = (probabilities * (prob_grad - row_inner)).astype(jnp.bfloat16)
    query_grad = (
        jnp.einsum("hqk,khd->qhd", score_grad, k_heads, preferred_element_type=jnp.float32)
        * score_scale
    )
    key_grad = (
        jnp.einsum("hqk,qhd->khd", score_grad, q_heads, preferred_element_type=jnp.float32)
        * score_scale
    )
    stacked = jnp.stack([query_grad, key_grad, value_grad], axis=1)
    return stacked.reshape(seq_len, 3, -1).astype(jnp.bfloat16)


def shards(
    tokens,
    cotangent,
    image_mask,
    qkv_weight,
    out_weight,
    up_weight,
    down_weight,
    qv_bias,
    up_bias,
    out_bias,
    down_bias,
    attn_gain,
    attn_shift,
    mlp_gain,
    mlp_shift,
):
    lane_count = lax.axis_size("tensor")
    lane_index = lax.axis_index("tensor")
    images_here, rows_here, model_width = tokens.shape
    seq_total = rows_here * lane_count
    head_part = qkv_weight.shape[3]
    hidden_part = up_weight.shape[2]
    hidden_total = hidden_part * lane_count
    layer_count = qkv_weight.shape[0]
    gathered_small = (
        lax.all_gather(qv_bias, ("dp", "tensor"), axis=2, tiled=True),
        lax.all_gather(up_bias, ("dp", "tensor"), axis=1, tiled=True),
        lax.all_gather(out_bias, ("dp", "tensor"), axis=1, tiled=True),
        lax.all_gather(down_bias, ("dp", "tensor"), axis=1, tiled=True),
        lax.all_gather(attn_gain, ("dp", "tensor"), axis=1, tiled=True),
        lax.all_gather(attn_shift, ("dp", "tensor"), axis=1, tiled=True),
        lax.all_gather(mlp_gain, ("dp", "tensor"), axis=1, tiled=True),
        lax.all_gather(mlp_shift, ("dp", "tensor"), axis=1, tiled=True),
    )
    qv_full, up_full, out_full, down_full, gain_one, shift_one, gain_two, shift_two = tuple(
        (member.astype(jnp.float32) for member in gathered_small)
    )
    qv_here = lax.dynamic_slice_in_dim(qv_full, lane_index * head_part, head_part, 2)
    up_here = lax.dynamic_slice_in_dim(up_full, lane_index * hidden_part, hidden_part, 1)
    key_valid = jnp.arange(seq_total) < VALID
    row_valid = lane_index * rows_here + jnp.arange(rows_here) < VALID
    stream = tokens.astype(jnp.float32)
    kept_weights = []
    kept_rows = []
    for layer_at in range(layer_count):
        weights = (
            lax.all_gather(qkv_weight[layer_at], "dp", axis=0, tiled=True),
            lax.all_gather(out_weight[layer_at], "dp", axis=0, tiled=True),
            lax.all_gather(up_weight[layer_at], "dp", axis=0, tiled=True),
            lax.all_gather(down_weight[layer_at], "dp", axis=0, tiled=True),
        )
        kept_weights.append(weights)
        qkv_full, proj_full, up_matrix, down_matrix = weights
        normed_one = layer_norm(stream, gain_one[layer_at], shift_one[layer_at]).astype(
            jnp.bfloat16
        )
        rows_one = spread_rows(normed_one)
        bias_three = jnp.stack(
            [qv_here[layer_at, 0], jnp.zeros_like(qv_here[layer_at, 0]), qv_here[layer_at, 1]]
        )
        projected = (
            jnp.einsum("isd,dce->isce", rows_one, qkv_full, preferred_element_type=jnp.float32)
            + bias_three
        )
        projected = projected.astype(jnp.bfloat16)
        queries = projected[:, :, 0]
        key_rows = projected[:, :, 1]
        value_rows = projected[:, :, 2]
        mixed_rows, log_total = lax.map(
            lambda block_in: attend_image(block_in, key_valid, HD), (queries, key_rows, value_rows)
        )
        attn_part = jnp.einsum(
            "ise,de->isd", mixed_rows, proj_full, preferred_element_type=jnp.float32
        )
        hidden = stream + branch_total(attn_part) + out_full[layer_at]
        normed_two = layer_norm(hidden, gain_two[layer_at], shift_two[layer_at]).astype(
            jnp.bfloat16
        )
        rows_two = spread_rows(normed_two)
        pre_act = (
            jnp.einsum("isd,df->isf", rows_two, up_matrix, preferred_element_type=jnp.float32)
            + up_here[layer_at]
        )
        activated = gelu_exact(pre_act).astype(jnp.bfloat16)
        down_part = jnp.einsum(
            "isf,df->isd", activated, down_matrix, preferred_element_type=jnp.float32
        )
        kept_rows.append(
            (
                stream,
                rows_one,
                queries,
                key_rows,
                value_rows,
                log_total,
                mixed_rows,
                hidden,
                rows_two,
                pre_act,
                activated,
            )
        )
        stream = hidden + branch_total(down_part) + down_full[layer_at]
    output = stream.astype(jnp.bfloat16)
    stream_grad = (
        cotangent.astype(jnp.float32)
        * image_mask.astype(jnp.float32)[:, None, None]
        * row_valid.astype(jnp.float32)[None, :, None]
    )
    weight_lists = [[None] * layer_count for member in range(4)]
    small_lists = [[None] * layer_count for member in range(8)]
    for layer_at in reversed(range(layer_count)):
        weights = (
            lax.all_gather(qkv_weight[layer_at], "dp", axis=0, tiled=True),
            lax.all_gather(out_weight[layer_at], "dp", axis=0, tiled=True),
            lax.all_gather(up_weight[layer_at], "dp", axis=0, tiled=True),
            lax.all_gather(down_weight[layer_at], "dp", axis=0, tiled=True),
        )
        qkv_full, proj_full, up_matrix, down_matrix = weights
        (
            stream_in,
            rows_one,
            queries,
            key_rows,
            value_rows,
            log_total,
            mixed_rows,
            hidden,
            rows_two,
            pre_act,
            activated,
        ) = kept_rows[layer_at]
        down_bias_part = jnp.sum(stream_grad, axis=(0, 1))
        grad_rows_one = gather_grads(stream_grad.astype(jnp.bfloat16))
        down_grad = jnp.einsum(
            "isd,isf->df", grad_rows_one, activated, preferred_element_type=jnp.float32
        )
        act_grad = jnp.einsum(
            "isd,df->isf", grad_rows_one, down_matrix, preferred_element_type=jnp.float32
        )
        unused_value, gelu_pull = jax.vjp(gelu_exact, pre_act)
        pre_grad = gelu_pull(act_grad)[0].astype(jnp.bfloat16)
        up_bias_part = jnp.sum(pre_grad, axis=(0, 1), dtype=jnp.float32)
        up_grad = jnp.einsum("isd,isf->df", rows_two, pre_grad, preferred_element_type=jnp.float32)
        normed_two_grad = grad_total(
            jnp.einsum("isf,df->isd", pre_grad, up_matrix, preferred_element_type=jnp.float32)
        )
        unused_value, norm_pull = jax.vjp(
            layer_norm, hidden, gain_two[layer_at], shift_two[layer_at]
        )
        hidden_grad, gain_two_grad, shift_two_grad = norm_pull(normed_two_grad)
        hidden_grad = hidden_grad + stream_grad
        out_bias_part = jnp.sum(hidden_grad, axis=(0, 1))
        grad_rows_two = gather_grads(hidden_grad.astype(jnp.bfloat16))
        proj_grad = jnp.einsum(
            "isd,ise->de", grad_rows_two, mixed_rows, preferred_element_type=jnp.float32
        )
        mixed_grad = jnp.einsum(
            "isd,de->ise", grad_rows_two, proj_full, preferred_element_type=jnp.float32
        ).astype(jnp.bfloat16)
        qkv_rows_grad = lax.map(
            lambda block_in: attend_back_image(block_in, key_valid, HD),
            (queries, key_rows, value_rows, log_total, mixed_grad),
        )
        qv_part = jnp.sum(qkv_rows_grad[:, :, 0::2], axis=(0, 1), dtype=jnp.float32)
        qkv_grad = jnp.einsum(
            "isd,isce->dce", rows_one, qkv_rows_grad, preferred_element_type=jnp.float32
        )
        normed_one_grad = grad_total(
            jnp.einsum("isce,dce->isd", qkv_rows_grad, qkv_full, preferred_element_type=jnp.float32)
        )
        unused_value, norm_pull = jax.vjp(
            layer_norm, stream_in, gain_one[layer_at], shift_one[layer_at]
        )
        input_part, gain_one_grad, shift_one_grad = norm_pull(normed_one_grad)
        stream_grad = hidden_grad + input_part
        owned = (
            lax.psum_scatter(qkv_grad, "dp", scatter_dimension=0, tiled=True),
            lax.psum_scatter(proj_grad, "dp", scatter_dimension=0, tiled=True),
            lax.psum_scatter(up_grad, "dp", scatter_dimension=0, tiled=True),
            lax.psum_scatter(down_grad, "dp", scatter_dimension=0, tiled=True),
        )
        for member in range(4):
            weight_lists[member][layer_at] = owned[member]
        qv_whole = lax.dynamic_update_slice_in_dim(
            jnp.zeros((2, model_width), jnp.float32), qv_part, lane_index * head_part, 1
        )
        up_whole = lax.dynamic_update_slice_in_dim(
            jnp.zeros((hidden_total,), jnp.float32), up_bias_part, lane_index * hidden_part, 0
        )
        small_parts = (
            qv_whole,
            up_whole,
            out_bias_part,
            down_bias_part,
            gain_one_grad,
            shift_one_grad,
            gain_two_grad,
            shift_two_grad,
        )
        for member in range(8):
            small_lists[member][layer_at] = small_parts[member]
    stacked_small = [jnp.stack(entries) for entries in small_lists]
    small_grads = (
        lax.psum_scatter(stacked_small[0], ("dp", "tensor"), scatter_dimension=2, tiled=True),
        lax.psum_scatter(stacked_small[1], ("dp", "tensor"), scatter_dimension=1, tiled=True),
        lax.psum_scatter(stacked_small[2], ("dp", "tensor"), scatter_dimension=1, tiled=True),
        lax.psum_scatter(stacked_small[3], ("dp", "tensor"), scatter_dimension=1, tiled=True),
        lax.psum_scatter(stacked_small[4], ("dp", "tensor"), scatter_dimension=1, tiled=True),
        lax.psum_scatter(stacked_small[5], ("dp", "tensor"), scatter_dimension=1, tiled=True),
        lax.psum_scatter(stacked_small[6], ("dp", "tensor"), scatter_dimension=1, tiled=True),
        lax.psum_scatter(stacked_small[7], ("dp", "tensor"), scatter_dimension=1, tiled=True),
    )
    stacked_weights = tuple((jnp.stack(entries) for entries in weight_lists))
    return (
        output,
        stream_grad,
        stacked_weights[0],
        stacked_weights[1],
        stacked_weights[2],
        stacked_weights[3],
        small_grads[0],
        small_grads[1],
        small_grads[2],
        small_grads[3],
        small_grads[4],
        small_grads[5],
        small_grads[6],
        small_grads[7],
    )


def solution(mesh):
    return jax.shard_map(
        shards,
        mesh=mesh,
        in_specs=(
            P("dp", "tensor", None),
            P("dp", "tensor", None),
            P("dp"),
            P(None, "dp", None, "tensor"),
            P(None, "dp", "tensor"),
            P(None, "dp", "tensor"),
            P(None, "dp", "tensor"),
            P(None, None, ("dp", "tensor")),
            P(None, ("dp", "tensor")),
            P(None, ("dp", "tensor")),
            P(None, ("dp", "tensor")),
            P(None, ("dp", "tensor")),
            P(None, ("dp", "tensor")),
            P(None, ("dp", "tensor")),
            P(None, ("dp", "tensor")),
        ),
        out_specs=(
            P("dp", "tensor", None),
            P("dp", "tensor", None),
            P(None, "dp", None, "tensor"),
            P(None, "dp", "tensor"),
            P(None, "dp", "tensor"),
            P(None, "dp", "tensor"),
            P(None, None, ("dp", "tensor")),
            P(None, ("dp", "tensor")),
            P(None, ("dp", "tensor")),
            P(None, ("dp", "tensor")),
            P(None, ("dp", "tensor")),
            P(None, ("dp", "tensor")),
            P(None, ("dp", "tensor")),
            P(None, ("dp", "tensor")),
        ),
        check_vma=False,
    )
```

profile of v0, /device:TPU:0, one launch (start us, length us, event | category | flops | bytes accessed | tf_op | source)
XLA Modules:
  0.0 2694.3 jit_solution(6883718702961570361)
XLA Ops:
  9.3 69.5 %all-gather.8 = bf16[32,32,2]{1,2,0:T(2,128)(2,1)S(1)} all-gather(bf16[1,32,2]{1,2,0:T(2,128)(2,1)} %bitcast.498), channel_id=1, replica_groups=mesh['dp'=8,'tensor'=4] {'dp','tensor'}, dimensions={0}, use_global_device_ids=true | all-gather | bytes 4224 | tf_op jit(solution)/shard_map/all_gather | solution.py:135
  78.9 63.2 %all-gather.9 = bf16[32,32,2]{1,2,0:T(2,128)(2,1)S(1)} all-gather(bf16[1,32,2]{1,2,0:T(2,128)(2,1)} %bitcast.499), channel_id=1, replica_groups=mesh['dp'=8,'tensor'=4] {'dp','tensor'}, dimensions={0}, use_global_device_ids=true | all-gather | bytes 4224 | tf_op jit(solution)/shard_map/all_gather | solution.py:136
  148.8 65.8 %all-gather.10 = bf16[32,32,2]{1,2,0:T(2,128)(2,1)S(1)} all-gather(bf16[1,32,2]{1,2,0:T(2,128)(2,1)S(1)} %bitcast.500), channel_id=1, replica_groups=mesh['dp'=8,'tensor'=4] {'dp','tensor'}, dimensions={0}, use_global_device_ids=true | all-gather | bytes 4224 | tf_op jit(solution)/shard_map/all_gather | solution.py:133
  215.2 63.2 %all-gather.11 = bf16[32,32,2]{1,2,0:T(2,128)(2,1)S(1)} all-gather(bf16[1,32,2]{1,2,0:T(2,128)(2,1)S(1)} %bitcast.501), channel_id=1, replica_groups=mesh['dp'=8,'tensor'=4] {'dp','tensor'}, dimensions={0}, use_global_device_ids=true | all-gather | bytes 4224 | tf_op jit(solution)/shard_map/all_gather | solution.py:137
  278.5 65.0 %all-gather.12 = bf16[32,32,2]{1,2,0:T(2,128)(2,1)S(1)} all-gather(bf16[1,32,2]{1,2,0:T(2,128)(2,1)S(1)} %bitcast.502), channel_id=1, replica_groups=mesh['dp'=8,'tensor'=4] {'dp','tensor'}, dimensions={0}, use_global_device_ids=true | all-gather | bytes 4224 | tf_op jit(solution)/shard_map/all_gather | solution.py:138
  343.7 68.2 %all_gather.84 = bf16[2,2,1024]{1,0,2:T(2,128)(2,1)S(1)} all-gather(bf16[2,2,32]{1,0,2:T(2,128)(2,1)S(1)} %copy.172), channel_id=1, replica_groups=mesh['dp'=8,'tensor'=4] {'dp','tensor'}, dimensions={2}, use_global_device_ids=true | all-gather | bytes 8448 | tf_op jit(solution)/shard_map/all_gather | solution.py:131
  415.2 9.2 all-gather.1
  435.2 27.6 %fusion = bf16[152,1024]{1,0:T(8,128)(2,1)S(1)} fusion(bf16[1,584,1024]{2,1,0:T(8,128)(2,1)S(1)} %fusion.76), kind=kCustom, calls=%all-reduce-scatter | all-reduce-scatter fusion | flops 622593 | bytes 1507840
  474.3 65.8 %all_gather.91 = bf16[2,4096]{1,0:T(2,128)(2,1)S(1)} all-gather(bf16[2,128]{1,0:T(2,128)(2,1)S(1)} %copy-done.65), channel_id=1, replica_groups=mesh['dp'=8,'tensor'=4] {'dp','tensor'}, dimensions={1}, use_global_device_ids=true | all-gather | bytes 16896 | tf_op jit(solution)/shard_map/all_gather | solution.py:132
  540.7 63.4 %all-gather.13 = bf16[32,32,2]{1,2,0:T(2,128)(2,1)S(1)} all-gather(bf16[1,32,2]{1,2,0:T(2,128)(2,1)S(1)} %bitcast.503), channel_id=1, replica_groups=mesh['dp'=8,'tensor'=4] {'dp','tensor'}, dimensions={0}, use_global_device_ids=true | all-gather | bytes 4224 | tf_op jit(solution)/shard_map/all_gather | solution.py:134
  604.2 5.6 multiply_convert_fusion.3
  609.9 3.4 fusion.64
  613.3 24.4 fusion.1
  646.8 10.8 all-gather.5
  657.6 38.7 %all-gather.33.cloned.1.call-done = bf16[1,584,1024]{2,0,1:T(2,128)(2,1)} async-done(((bf16[1,146,1024]{2,0,1:T(2,128)(2,1)}), bf16[1,584,1024]{2,0,1:T(2,128)(2,1)}) %all-gather.33.cloned.1.call-update) | async-done | bytes 1196048 | tf_op jit(solution)/shard_map/all_gather | solution.py:28
  711.6 27.6 %fusion.2 = bf16[152,1024]{1,0:T(8,128)(2,1)S(1)} fusion(bf16[1,584,1024]{2,1,0:T(8,128)(2,1)} %fusion.77), kind=kCustom, calls=%all-reduce-scatter.2 | all-reduce-scatter fusion | flops 622593 | bytes 1507840
  746.7 4.3 fusion.175
  759.3 49.1 %all-gather.35.cloned.1.call-done = bf16[1,584,1024]{2,0,1:T(2,128)(2,1)} async-done(((bf16[1,146,1024]{2,0,1:T(2,128)(2,1)}), bf16[1,584,1024]{2,0,1:T(2,128)(2,1)}) %all-gather.35.cloned.1.call-update) | async-done | bytes 1196048 | tf_op jit(solution)/shard_map/all_gather | solution.py:28
  808.3 5.7 multiply_convert_fusion.2
  814.0 22.8 all-gather.55.cloned.1.call-done
  836.8 53.2 %all-gather.37.cloned.1.call-done = bf16[1,584,1024]{2,0,1:T(2,128)(2,1)} async-done(((bf16[1,146,1024]{2,0,1:T(2,128)(2,1)}), bf16[1,584,1024]{2,0,1:T(2,128)(2,1)}) %all-gather.37.cloned.1.call-update) | async-done | bytes 1196048 | tf_op jit(solution)/shard_map/all_gather | solution.py:32
  890.0 6.1 convert_reduce_fusion
  899.6 28.2 %fusion.4 = bf16[152,1024]{1,0:T(8,128)(2,1)} fusion(bf16[1,584,1024]{2,1,0:T(8,128)(2,1)} %fusion.61), kind=kCustom, calls=%all-reduce-scatter.4 | all-reduce-scatter fusion | flops 622593 | bytes 1507840
  932.2 4.1 concatenate.28
  937.4 4.0 multiply_reduce_fusion.2
  948.8 50.5 %all-gather.39.cloned.1.call-done = bf16[1,584,1024]{2,0,1:T(2,128)(2,1)} async-done(((bf16[1,146,1024]{2,0,1:T(2,128)(2,1)}), bf16[1,584,1024]{2,0,1:T(2,128)(2,1)}) %all-gather.39.cloned.1.call-update) | async-done | bytes 1196048 | tf_op jit(solution)/shard_map/all_gather | solution.py:32
  1001.7 3.9 fusion.92
  1005.6 4.1 multiply_reduce_fusion.1
  1017.0 3.9 fusion.70
  1020.8 28.4 %fusion.5 = bf16[152,1024]{1,0:T(8,128)(2,1)} fusion(bf16[1,584,1024]{2,1,0:T(8,128)(2,1)} %fusion.70), kind=kCustom, calls=%all-reduce-scatter.5 | all-reduce-scatter fusion | flops 622593 | bytes 1507840
  1065.7 50.9 %all-gather.41.cloned.1.call-done = bf16[1,584,1024]{2,0,1:T(2,128)(2,1)} async-done(((bf16[1,146,1024]{2,0,1:T(2,128)(2,1)}), bf16[1,584,1024]{2,0,1:T(2,128)(2,1)}) %all-gather.41.cloned.1.call-update) | async-done | bytes 1196048 | tf_op jit(solution)/shard_map/all_gather | solution.py:32
  1116.6 5.5 convert_reduce_fusion.1
  1125.6 27.7 %fusion.6 = bf16[152,1024]{1,0:T(8,128)(2,1)S(1)} fusion(bf16[1,584,1024]{2,1,0:T(8,128)(2,1)} %fusion.67), kind=kCustom, calls=%all-reduce-scatter.6 | all-reduce-scatter fusion | flops 622593 | bytes 1507840
  1165.0 4.4 fusion.58
  1176.9 39.3 %all-gather.43.cloned.1.call-done = bf16[1,584,1024]{2,0,1:T(2,128)(2,1)} async-done(((bf16[1,146,1024]{2,0,1:T(2,128)(2,1)}), bf16[1,584,1024]{2,0,1:T(2,128)(2,1)}) %all-gather.43.cloned.1.call-update) | async-done | bytes 1196048 | tf_op jit(solution)/shard_map/all_gather | solution.py:32
  1218.6 3.9 fusion.95
  1222.5 4.1 multiply_reduce_fusion
  1231.2 3.6 fusion.73
  1234.8 50.9 %fusion.173 = (bf16[152,1024]{1,0:T(8,128)(2,1)S(1)}, bf16[152,1024]{1,0:T(8,128)(2,1)S(1)}) fusion(bf16[1,584,1024]{2,1,0:T(8,128)(2,1)} %fusion.58, bf16[1,584,1024]{2,1,0:T(8,128)(2,1)} %fusion.73), kind=kCustom, calls=%all-reduce-scatter.8 | all-reduce-scatter fusion | flops 1245185 | bytes 3015168
  1297.1 3.4 fusion.106
  1300.7 3.4 fusion.100
  1304.4 5.9 fusion.109
  1310.4 6.0 fusion.103
  1316.5 6.0 fusion.112
  1322.5 5.9 fusion.118
  1329.5 4.9 fusion.115
  1335.5 4.9 fusion.121
  1340.4 3.6 collective-permute-start.3
  1344.1 9.4 reduce-scatter.79.cloned.1.call-done
  1354.9 131.7 %reduce-scatter.87.cloned.1.call-done = f32[32,2]{1,0:T(8,128)} async-done(((f32[1024,2]{1,0:T(8,128)}), f32[32,2]{1,0:T(8,128)}) %reduce-scatter.87.cloned.1.call-update) | async-done | bytes 272
  1488.0 131.5 %reduce-scatter.77.cloned.1.call-done = f32[32,2]{1,0:T(8,128)} async-done(((f32[1024,2]{1,0:T(8,128)}), f32[32,2]{1,0:T(8,128)}) %reduce-scatter.77.cloned.1.call-update) | async-done | bytes 272
  1620.8 131.6 %reduce-scatter.85.cloned.1.call-done = f32[32,2]{1,0:T(8,128)} async-done(((f32[1024,2]{1,0:T(8,128)}), f32[32,2]{1,0:T(8,128)}) %reduce-scatter.85.cloned.1.call-update) | async-done | bytes 272
  1753.8 135.4 %reduce-scatter.75.cloned.1.call-done = f32[128,2]{1,0:T(8,128)} async-done(((f32[4096,2]{1,0:T(8,128)}), f32[128,2]{1,0:T(8,128)}) %reduce-scatter.75.cloned.1.call-update) | async-done | bytes 1040
  1890.7 133.8 %reduce-scatter.73.cloned.1.call-done = f32[32,4]{1,0:T(8,128)} async-done(((f32[1024,4]{1,0:T(8,128)}), f32[32,4]{1,0:T(8,128)}) %reduce-scatter.73.cloned.1.call-update) | async-done | bytes 528
  2031.9 125.6 %reduce-scatter.83.cloned.1.call-done = f32[32,2]{1,0:T(8,128)} async-done(((f32[1024,2]{1,0:T(8,128)}), f32[32,2]{1,0:T(8,128)}) %reduce-scatter.83.cloned.1.call-update) | async-done | bytes 272
  2158.9 131.7 %reduce-scatter.81.cloned.1.call-done = f32[32,2]{1,0:T(8,128)} async-done(((f32[1024,2]{1,0:T(8,128)}), f32[32,2]{1,0:T(8,128)}) %reduce-scatter.81.cloned.1.call-update) | async-done | bytes 272
  2292.0 34.8 %reduce-scatter.63.cloned.1.call-done = f32[128,256]{1,0:T(8,128)} async-done(((f32[1024,256]{1,0:T(8,128)}), f32[128,256]{1,0:T(8,128)}) %reduce-scatter.63.cloned.1.call-update) | async-done | bytes 131088 | tf_op jit(solution)/shard_map/reduce_scatter | solution.py:284
  2326.7 39.6 %reduce-scatter.61.cloned.1.call-done = f32[128,256]{1,0:T(8,128)} async-done(((f32[1024,256]{1,0:T(8,128)}), f32[128,256]{1,0:T(8,128)}) %reduce-scatter.61.cloned.1.call-update) | async-done | bytes 131088 | tf_op jit(solution)/shard_map/reduce_scatter | solution.py:284
  2368.0 53.0 %reduce-scatter.71.cloned.1.call-done = f32[128,1024]{1,0:T(8,128)} async-done(((f32[1024,1024]{1,0:T(8,128)}), f32[128,1024]{1,0:T(8,128)}) %reduce-scatter.71.cloned.1.call-update) | async-done | bytes 524304 | tf_op jit(solution)/shard_map/reduce_scatter | solution.py:286
  2421.0 54.9 %reduce-scatter.69.cloned.1.call-done = f32[128,1024]{1,0:T(8,128)} async-done(((f32[1024,1024]{1,0:T(8,128)}), f32[128,1024]{1,0:T(8,128)}) %reduce-scatter.69.cloned.1.call-update) | async-done | bytes 524304 | tf_op jit(solution)/shard_map/reduce_scatter | solution.py:286
  2478.3 52.2 %reduce-scatter.67.cloned.1.call-done = f32[128,1024]{1,0:T(8,128)} async-done(((f32[1024,1024]{1,0:T(8,128)}), f32[128,1024]{1,0:T(8,128)}) %reduce-scatter.67.cloned.1.call-update) | async-done | bytes 524304 | tf_op jit(solution)/shard_map/reduce_scatter | solution.py:285
  2530.5 55.1 %reduce-scatter.65.cloned.1.call-done = f32[128,1024]{1,0:T(8,128)} async-done(((f32[1024,1024]{1,0:T(8,128)}), f32[128,1024]{1,0:T(8,128)}) %reduce-scatter.65.cloned.1.call-update) | async-done | bytes 524304 | tf_op jit(solution)/shard_map/reduce_scatter | solution.py:285
  2587.9 47.3 %reduce-scatter.59.cloned.1.call-done = f32[128,3,256]{2,0,1:T(8,128)} async-done(((f32[1024,3,256]{2,0,1:T(8,128)}), f32[128,3,256]{2,0,1:T(8,128)}) %reduce-scatter.59.cloned.1.call-update) | async-done | bytes 393232 | tf_op jit(solution)/shard_map/reduce_scatter | solution.py:283
  2635.2 49.8 %reduce-scatter.57.cloned.1.call-done = f32[128,3,256]{2,0,1:T(8,128)} async-done(((f32[1024,3,256]{2,0,1:T(8,128)}), f32[128,3,256]{2,0,1:T(8,128)}) %reduce-scatter.57.cloned.1.call-update) | async-done | bytes 393232 | tf_op jit(solution)/shard_map/reduce_scatter | solution.py:283
  (415 shorter events, 185.2 us)
Async XLA Ops:
  7.2 139.7 %copy-start.27 = (bf16[2,128,3,256]{3,1,2,0:T(8,128)(2,1)S(1)}, bf16[2,128,3,256]{3,1,2,0:T(8,128)(2,1)}, u32[]{:S(2)}) copy-start(bf16[2,128,3,256]{3,1,2,0:T(8,128)(2,1)} %param.18) | copy-start | bytes 1179652
  7.2 140.5 %copy-start.25 = (bf16[2,128,1024]{2,1,0:T(8,128)(2,1)S(1)}, bf16[2,128,1024]{2,1,0:T(8,128)(2,1)}, u32[]{:S(2)}) copy-start(bf16[2,128,1024]{2,1,0:T(8,128)(2,1)} %param.20) | copy-start | bytes 1572868
  7.2 417.4 %all-gather.29.cloned.1.call-start = ((), (), s32[]{:S(2)}) async-start(), calls=%async_computation.16 | async-start | bytes 2990080 | tf_op jit(solution)/shard_map/all_gather | solution.py:28
  142.2 73.0 %copy-start.63 = (bf16[2,32]{1,0:T(2,128)(2,1)S(1)}, bf16[2,32]{1,0:T(2,128)(2,1)}, u32[]{:S(2)}) copy-start(bf16[2,32]{1,0:T(2,128)(2,1)} %param.28) | copy-start | bytes 388
  145.1 266.8 %copy-start.51 = (f32[146]{0:T(256)}, f32[146]{0:T(256)S(1)}, u32[]{:S(2)}) copy-start(f32[146]{0:T(256)S(1)} %get-tuple-element.222) | copy-start | bytes 1756
  145.1 133.4 %copy-start.64 = (bf16[2,32]{1,0:T(2,128)(2,1)S(1)}, bf16[2,32]{1,0:T(2,128)(2,1)}, u32[]{:S(2)}) copy-start(bf16[2,32]{1,0:T(2,128)(2,1)} %param.29) | copy-start | bytes 388
  145.2 198.5 %copy-start.35 = (bf16[2,128,256]{2,1,0:T(8,128)(2,1)S(1)}, bf16[2,128,256]{2,1,0:T(8,128)(2,1)}, u32[]{:S(2)}) copy-start(bf16[2,128,256]{2,1,0:T(8,128)(2,1)} %param.19) | copy-start | bytes 393220
  145.2 266.7 %copy-start.44 = (f32[146]{0:T(256)}, f32[146]{0:T(256)S(1)}, u32[]{:S(2)}) copy-start(f32[146]{0:T(256)S(1)} %fusion.165) | copy-start | bytes 1756
  146.8 277.8 %all-gather.45.cloned.1.call-start = ((), (), s32[]{:S(2)}) async-start(), calls=%async_computation.32 | async-start | bytes 1769472 | tf_op jit(solution)/shard_map/all_gather | solution.py:152
  147.6 456.6 %all-gather.47.cloned.1.call-start = ((), (), s32[]{:S(2)}) async-start(), calls=%async_computation.33 | async-start | bytes 2359296 | tf_op jit(solution)/shard_map/all_gather | solution.py:154
  148.6 455.7 %all-gather.31.cloned.1.call-start = ((), (), s32[]{:S(2)}) async-start(), calls=%async_computation.17 | async-start | bytes 2990080 | tf_op jit(solution)/shard_map/all_gather | solution.py:28
  424.4 9.5 copy-start.14
  433.9 32.2 %copy-start.67 = (u32[32]{0:T(128)S(1)}, u32[32]{0:T(128)}, u32[]{:S(2)}) copy-start(u32[32]{0:T(128)} %constant.140) | copy-start | bytes 388
  434.6 33.3 %copy-start.13 = (bf16[1,146,1024]{2,1,0:T(8,128)(2,1)S(1)}, bf16[1,146,1024]{2,1,0:T(8,128)(2,1)}, u32[]{:S(2)}) copy-start(bf16[1,146,1024]{2,1,0:T(8,128)(2,1)} %param.15) | copy-start | bytes 897028
  462.8 4.5 collective-permute-start
  469.1 71.5 %copy-start.66 = (bf16[2,32]{1,0:T(2,128)(2,1)S(1)}, bf16[2,32]{1,0:T(2,128)(2,1)}, u32[]{:S(2)}) copy-start(bf16[2,32]{1,0:T(2,128)(2,1)} %param.25) | copy-start | bytes 388
  471.1 138.8 %copy-start.53 = (f32[146]{0:T(256)}, f32[146]{0:T(256)S(1)}, u32[]{:S(2)}) copy-start(f32[146]{0:T(256)S(1)} %get-tuple-element.218) | copy-start | bytes 1756
  471.1 69.0 %copy-start.46 = (f32[146]{0:T(256)}, f32[146]{0:T(256)S(1)}, u32[]{:S(2)}) copy-start(f32[146]{0:T(256)S(1)} %fusion.166) | copy-start | bytes 1756
  472.7 137.2 %all-gather.49.cloned.1.call-start = ((), (), s32[]{:S(2)}) async-start(), calls=%async_computation.34 | async-start | bytes 2359296 | tf_op jit(solution)/shard_map/all_gather | solution.py:155
  473.6 184.0 %all-gather.51.cloned.1.call-start = ((), (), s32[]{:S(2)}) async-start(), calls=%async_computation.35 | async-start | bytes 1769472 | tf_op jit(solution)/shard_map/all_gather | solution.py:152
  474.2 222.1 %all-gather.33.cloned.1.call-start = ((), (), s32[]{:S(2)}) async-start(), calls=%async_computation.18 | async-start | bytes 2990080 | tf_op jit(solution)/shard_map/all_gather | solution.py:28
  540.7 69.2 %copy-start.59 = (f32[1,1024]{1,0:T(1,128)}, f32[1,1024]{1,0:T(1,128)S(1)}, u32[]{:S(2)}) copy-start(f32[1,1024]{1,0:T(1,128)S(1)} %get-tuple-element.241) | copy-start | bytes 12292
  637.8 3.1 collective-permute-start.1
  644.4 55.2 %copy-start.55 = (f32[146]{0:T(256)}, f32[146]{0:T(256)S(1)}, u32[]{:S(2)}) copy-start(f32[146]{0:T(256)S(1)} %get-tuple-element.214) | copy-start | bytes 1756
  644.4 55.2 %copy-start.48 = (f32[146]{0:T(256)}, f32[146]{0:T(256)S(1)}, u32[]{:S(2)}) copy-start(f32[146]{0:T(256)S(1)} %fusion.167) | copy-start | bytes 1756
  646.0 113.2 %all-gather.53.cloned.1.call-start = ((), (), s32[]{:S(2)}) async-start(), calls=%async_computation.36 | async-start | bytes 2359296 | tf_op jit(solution)/shard_map/all_gather | solution.py:154
  646.8 161.5 %all-gather.35.cloned.1.call-start = ((), (), s32[]{:S(2)}) async-start(), calls=%async_computation.19 | async-start | bytes 2990080 | tf_op jit(solution)/shard_map/all_gather | solution.py:28
  739.2 3.6 collective-permute-start.2
  757.1 79.7 %all-gather.55.cloned.1.call-start = ((), (), s32[]{:S(2)}) async-start(), calls=%async_computation.37 | async-start | bytes 2359296 | tf_op jit(solution)/shard_map/all_gather | solution.py:155
  757.7 132.3 %all-gather.37.cloned.1.call-start = ((), (), s32[]{:S(2)}) async-start(), calls=%async_computation.20 | async-start | bytes 2990080 | tf_op jit(solution)/shard_map/all_gather | solution.py:32
  759.0 240.3 %all-gather.39.cloned.1.call-start = ((), (), s32[]{:S(2)}) async-start(), calls=%async_computation.21 | async-start | bytes 2990080 | tf_op jit(solution)/shard_map/all_gather | solution.py:32
  928.6 3.6 collective-permute-start.4
  947.9 168.7 %all-gather.41.cloned.1.call-start = ((), (), s32[]{:S(2)}) async-start(), calls=%async_computation.22 | async-start | bytes 2990080 | tf_op jit(solution)/shard_map/all_gather | solution.py:32
  1001.7 8.0 slice-start.2
  1020.8 37.1 %copy-start.49 = (f32[146]{0:T(256)S(1)}, f32[146]{0:T(256)}, u32[]{:S(2)}) copy-start(f32[146]{0:T(256)} %copy-done.48) | copy-start | bytes 1756
  1020.8 39.9 %copy-start.56 = (f32[146]{0:T(256)S(1)}, f32[146]{0:T(256)}, u32[]{:S(2)}) copy-start(f32[146]{0:T(256)} %copy-done.55) | copy-start | bytes 1756
  1050.0 3.6 collective-permute-start.5
  1060.8 55.8 %copy-start.60 = (f32[1,1024]{1,0:T(1,128)S(1)}, f32[1,1024]{1,0:T(1,128)}, u32[]{:S(2)}) copy-start(f32[1,1024]{1,0:T(1,128)} %copy-done.59) | copy-start | bytes 12292
  1065.3 150.9 %all-gather.43.cloned.1.call-start = ((), (), s32[]{:S(2)}) async-start(), calls=%async_computation.23 | async-start | bytes 2990080 | tf_op jit(solution)/shard_map/all_gather | solution.py:32
  1125.6 31.9 %copy-start.47 = (f32[146]{0:T(256)S(1)}, f32[146]{0:T(256)}, u32[]{:S(2)}) copy-start(f32[146]{0:T(256)} %copy-done.46) | copy-start | bytes 1756
  1125.6 34.7 %copy-start.54 = (f32[146]{0:T(256)S(1)}, f32[146]{0:T(256)}, u32[]{:S(2)}) copy-start(f32[146]{0:T(256)} %copy-done.53) | copy-start | bytes 1756
  1153.3 3.6 collective-permute-start.6
  1164.8 188.7 %reduce-scatter.79.cloned.1.call-start = ((), (), s32[]{:S(2)}) async-start(), calls=%async_computation.41 | async-start | bytes 540672
  1171.1 315.5 %reduce-scatter.87.cloned.1.call-start = ((), (), s32[]{:S(2)}) async-start(), calls=%async_computation.45 | async-start | bytes 540672
  1172.3 447.1 %reduce-scatter.77.cloned.1.call-start = ((), (), s32[]{:S(2)}) async-start(), calls=%async_computation.40 | async-start | bytes 540672
  1173.4 579.0 %reduce-scatter.85.cloned.1.call-start = ((), (), s32[]{:S(2)}) async-start(), calls=%async_computation.44 | async-start | bytes 540672
  1174.6 41.6 %copy-start.15 = (bf16[1,1024,256]{2,1,0:T(8,128)(2,1)S(1)}, bf16[1,1024,256]{2,1,0:T(8,128)(2,1)}, u32[]{:S(2)}) copy-start(bf16[1,1024,256]{2,1,0:T(8,128)(2,1)} %copy-done.14) | copy-start | bytes 1572868
  1174.6 714.6 %reduce-scatter.75.cloned.1.call-start = ((), (), s32[]{:S(2)}) async-start(), calls=%async_computation.39 | async-start | bytes 2162688
  1176.7 847.8 %reduce-scatter.73.cloned.1.call-start = ((), (), s32[]{:S(2)}) async-start(), calls=%async_computation.38 | async-start | bytes 540672
  1286.3 4.3 collective-permute-start.7
  1290.6 866.9 %reduce-scatter.83.cloned.1.call-start = ((), (), s32[]{:S(2)}) async-start(), calls=%async_computation.43 | async-start | bytes 540672
  1295.9 994.7 %reduce-scatter.81.cloned.1.call-start = ((), (), s32[]{:S(2)}) async-start(), calls=%async_computation.42 | async-start | bytes 540672
  1297.1 1029.6 %reduce-scatter.63.cloned.1.call-start = ((), (), s32[]{:S(2)}) async-start(), calls=%async_computation.27 | async-start | bytes 1179648 | tf_op jit(solution)/shard_map/reduce_scatter | solution.py:284
  1300.6 1065.8 %reduce-scatter.61.cloned.1.call-start = ((), (), s32[]{:S(2)}) async-start(), calls=%async_computation.26 | async-start | bytes 1179648 | tf_op jit(solution)/shard_map/reduce_scatter | solution.py:284
  1304.1 1116.9 %reduce-scatter.71.cloned.1.call-start = ((), (), s32[]{:S(2)}) async-start(), calls=%async_computation.31 | async-start | bytes 4718592 | tf_op jit(solution)/shard_map/reduce_scatter | solution.py:286
  1310.3 1165.6 %reduce-scatter.69.cloned.1.call-start = ((), (), s32[]{:S(2)}) async-start(), calls=%async_computation.30 | async-start | bytes 4718592 | tf_op jit(solution)/shard_map/reduce_scatter | solution.py:286
  1316.4 1214.1 %reduce-scatter.67.cloned.1.call-start = ((), (), s32[]{:S(2)}) async-start(), calls=%async_computation.29 | async-start | bytes 4718592 | tf_op jit(solution)/shard_map/reduce_scatter | solution.py:285
  1322.4 1263.2 %reduce-scatter.65.cloned.1.call-start = ((), (), s32[]{:S(2)}) async-start(), calls=%async_computation.28 | async-start | bytes 4718592 | tf_op jit(solution)/shard_map/reduce_scatter | solution.py:285
  1328.4 1306.8 %reduce-scatter.59.cloned.1.call-start = ((), (), s32[]{:S(2)}) async-start(), calls=%async_computation.25 | async-start | bytes 3538944 | tf_op jit(solution)/shard_map/reduce_scatter | solution.py:283
  1334.5 1350.6 %reduce-scatter.57.cloned.1.call-start = ((), (), s32[]{:S(2)}) async-start(), calls=%async_computation.24 | async-start | bytes 3538944 | tf_op jit(solution)/shard_map/reduce_scatter | solution.py:283
  1340.4 686.1 %copy-start.3 = (f32[1,146,1024]{2,0,1:T(1,128)S(1)}, f32[1,146,1024]{2,0,1:T(1,128)}, u32[]{:S(2)}) copy-start(f32[1,146,1024]{2,0,1:T(1,128)} %copy-done.2) | copy-start | bytes 1794052
  1340.4 686.1 %copy-start.39 = (f32[1,1024]{1,0:T(1,128)S(1)}, f32[1,1024]{1,0:T(1,128)}, u32[]{:S(2)}) copy-start(f32[1,1024]{1,0:T(1,128)} %get-tuple-element.238) | copy-start | bytes 12292
  1340.4 687.6 %copy-start.52 = (f32[146]{0:T(256)S(1)}, f32[146]{0:T(256)}, u32[]{:S(2)}) copy-start(f32[146]{0:T(256)} %copy-done.51) | copy-start | bytes 1756
  1340.4 685.5 %collective-permute-start.3 = (bf16[18,1024]{1,0:T(8,128)(2,1)S(1)}, bf16[18,1024]{1,0:T(8,128)(2,1)S(1)}, u32[]{:S(2)}, u32[]{:S(2)}) collective-permute-start(bf16[18,1024]{1,0:T(8,128)(2,1)S(1)} %slice.175), channel_id=1, source_target_pairs={{0,1},{1,2},{2,3},{4,5},{5,6},{6,7},{8,9},{9,10},{10,11},{12,13},{... | collective-permute-start | bytes 110600
  (50 other events, 144.1 us)
Sparse Core Ops, SparseCore 0:
  146.9 49.0 all-gather.28
  198.5 24.3 all-gather.44
  225.4 27.8 all-gather.46
  472.8 49.9 all-gather.30
  525.2 26.5 all-gather.48
  554.2 25.6 all-gather.50
  646.1 50.1 all-gather.32
  698.8 26.6 all-gather.52
  757.2 51.0 all-gather.34
  810.1 26.6 all-gather.54
  838.9 51.0 all-gather.36
  948.0 51.2 all-gather.38
  1065.4 51.1 all-gather.40
  1164.9 51.1 all-gather.42
  1218.2 135.2 reduce-scatter.78
  1355.7 130.8 reduce-scatter.86
  1488.7 130.7 reduce-scatter.76
  1621.6 130.7 reduce-scatter.84
  1754.7 134.4 reduce-scatter.74
  1891.9 132.5 reduce-scatter.72
  2026.7 130.7 reduce-scatter.82
  2159.8 130.7 reduce-scatter.80
  2294.4 32.3 reduce-scatter.62
  2330.3 35.9 reduce-scatter.60
  2369.7 51.2 reduce-scatter.70
  2424.6 51.3 reduce-scatter.68
  2479.2 51.2 reduce-scatter.66
  2534.2 51.3 reduce-scatter.64
  2589.0 46.1 reduce-scatter.58
  2638.8 46.2 reduce-scatter.56
where the time goes:
time: 2700 us; the launch traced here: 2690 us
  waiting for transfers between devices  1630 us (60%)
  blocking collectives  759 us (28%)
  matrix products  122 us (5%)
  local copies, waits for them, and re-layouts  72.8 us (3%)
  other arithmetic  72.5 us (3%)
    unnamed x46, waiting for transfers between devices  939 us
    unnamed x7, blocking collectives  215 us
    all_gather x4, waiting for transfers between devices, gather_grads(): return lax.all_gather(grad_low, 'tensor', axis=1, tiled=True)  194 us
    reduce_scatter x2, waiting for transfers between devices, shards(): lax.psum_scatter(down_grad, 'dp', scatter_dimension=0, tiled=True)  108 us
    reduce_scatter x2, waiting for transfers between devices, shards(): lax.psum_scatter(up_grad, 'dp', scatter_dimension=0, tiled=True)  107 us
    reduce_scatter x2, waiting for transfers between devices, shards(): lax.psum_scatter(qkv_grad, 'dp', scatter_dimension=0, tiled=True)  97.2 us
    all_gather x4, waiting for transfers between devices, spread_rows(): return lax.all_gather(normed, 'tensor', axis=1, tiled=True)  87.8 us
    reduce_scatter x2, waiting for transfers between devices, shards(): lax.psum_scatter(proj_grad, 'dp', scatter_dimension=0, tiled=True)  74.4 us
  transfers between devices with their start and end apart: 38, of which 28 were waited for; matrix products, arithmetic and copies ran while one was open for 11% of the time, Pallas kernels for 0%

commit v1 on v0

v1 whole, which is shorter than its diff:
```python
import functools

import jax
import jax.numpy as jnp
from jax import lax
from jax.experimental import pallas as pl
from jax.experimental.pallas import tpu as pltpu
from jax.sharding import PartitionSpec as P

HD = 64
VALID = 577
EPS = 1e-06
ROOT_HALF = 0.7071067811865476
INV_ROOT_2PI = 0.3989422804014327
FAR_BELOW = -1e30
MESH = pl.DeviceIdType.MESH
F32 = jnp.float32
BF16 = jnp.bfloat16
TILE = 32
NT = 256


def dot_nn(a, b):
    return lax.dot_general(a, b, (((1,), (0,)), ((), ())), preferred_element_type=F32)


def dot_nt(a, b):
    return lax.dot_general(a, b, (((1,), (1,)), ((), ())), preferred_element_type=F32)


def dot_tn(a, b):
    return lax.dot_general(a, b, (((0,), (0,)), ((), ())), preferred_element_type=F32)


def loop(n, body):
    def step(i, carry):
        body(i)
        return carry

    lax.fori_loop(0, n, step, 0)


def aligned(v, m):
    return pl.multiple_of(v, m)


def kernel(
    layers, rows_real,
    tok, cot, wsh, small_in,
    out_ref, ig_ref, gw_ref, sg,
    W, xs, gs, n1, n2, r1, r2, a1, a2, qkv, o, act, dgl,
    gb, hb, ub, ob, dqkv, dk_acc, dv_acc, acc,
    sendA, recvA, sendB, recvB, tokst, cotst, igst, igrecv,
    small, smrecv, smf, qb, sgrecv,
    recv1, recv2, recv4,
    s0s, s0r, s1s, s1r, s2s, s2r,
    as_, ar, bs, br, cs, cr,
    tks, tkr, cts, ctr, oss, osr, sms, smr, sgs, sgr,
    g1s, g1r, g2s, g2r, g4s, g4r,
):
    width = xs.shape[1]
    half = xs.shape[0]
    slot = half // 2
    rows_all = 2 * half
    kb = wsh.shape[1]
    blk = 2 * kb
    hq = o.shape[2]
    fq = act.shape[2]
    heads = hq // HD
    wn = width // NT

    dp = lax.axis_index("dp")
    z = lax.axis_index("tensor")
    base = (dp // 8) * 8
    d8 = dp % 8
    y, x, c = d8 // 4, (d8 // 2) % 2, d8 % 2
    zh, zl = z // 2, z % 2
    q = zl + 2 * c
    z2 = (z + 2) % 4
    home = c == zh

    def dev(yy, xx, cc, zz):
        return (base + yy * 4 + xx * 2 + cc, zz)

    sib = dev(y, x, 1 - c, z)
    xn = dev(y, 1 - x, c, z)
    yn = dev(1 - y, x, c, z)
    zp = dev(y, x, c, z + 1 - 2 * zl)
    far = dev(y, x, c, z2)
    swap = dev(y, x, zh, 2 * c + zl)
    swap_pair = dev(y, x, zh, 2 * c + 1 - zl)

    def rc(src, dst, ss, rs, to):
        return pltpu.make_async_remote_copy(
            src_ref=src, dst_ref=dst, send_sem=ss, recv_sem=rs,
            device_id=to, device_id_type=MESH)

    def wait(ref, sem):
        pltpu.make_async_copy(ref, ref, sem).wait()

    barrier = pltpu.get_barrier_semaphore()
    greet = [xn, yn, sib]
    for k in range(1, 4):
        for cc in range(2):
            greet.append(dev(y, x, cc, (z + k) % 4))
    for to in greet:
        pl.semaphore_signal(barrier, inc=1, device_id=to, device_id_type=MESH)
    pl.semaphore_wait(barrier, len(greet))

    def rows_of(yy, xx):
        return aligned((2 * yy + xx) * blk, blk)

    my_rows = pl.ds(aligned(d8 * kb, kb), kb)
    own_blk = rows_of(y, x)
    x_blk = rows_of(y, 1 - x)
    y_blk = rows_of(1 - y, x)
    diag_blk = rows_of(1 - y, 1 - x)

    def s0_start(u):
        rc(wsh.at[u], W.at[u, my_rows], s0s.at[u, 0], s0r.at[u, c], dev(y, x, zh, z2)).start()

        @pl.when(home)
        def _():
            pltpu.make_async_copy(wsh.at[u], W.at[u, my_rows], s0r.at[u, c]).start()

        @pl.when(jnp.logical_not(home))
        def _():
            rc(wsh.at[u], W.at[u, my_rows], s0s.at[u, 1], s0r.at[u, c], sib).start()

    def s0_wait(u):
        for j in range(2):
            wait(W.at[u, pl.ds(own_blk + j * kb, kb)], s0r.at[u, j])

    def s1_start(u):
        ref = W.at[u, pl.ds(own_blk, blk)]
        rc(ref, ref, s1s.at[u, 0], s1r.at[u, 0], xn).start()
        rc(ref, ref, s1s.at[u, 1], s1r.at[u, 1], yn).start()

    def s1_wait(u):
        wait(W.at[u, pl.ds(x_blk, blk)], s1r.at[u, 0])
        wait(W.at[u, pl.ds(y_blk, blk)], s1r.at[u, 1])

    def s2_start(u):
        ref = W.at[u, pl.ds(x_blk, kb)]
        rc(ref, ref, s2s.at[u, 1], s2r.at[u, 1], yn).start()
        ref = W.at[u, pl.ds(y_blk + kb, kb)]
        rc(ref, ref, s2s.at[u, 0], s2r.at[u, 0], xn).start()

    def s2_wait(u):
        wait(W.at[u, pl.ds(diag_blk, kb)], s2r.at[u, 1])
        wait(W.at[u, pl.ds(diag_blk + kb, kb)], s2r.at[u, 0])

    def sends_done(u):
        ref = W.at[u, pl.ds(own_blk, kb)]
        wait(ref, s0s.at[u, 0])

        @pl.when(jnp.logical_not(home))
        def _():
            wait(ref, s0s.at[u, 1])

        for j in range(2):
            wait(W.at[u, pl.ds(own_blk, blk)], s1s.at[u, j])
            wait(ref, s2s.at[u, j])

    units = 3 * layers

    def pump(u):
        s1_wait(u)
        s2_start(u)
        if u + 1 < units:
            s0_wait(u + 1)
            s1_start(u + 1)
        if u >= 1 and u + 2 < units:
            s0_start(u + 2)

    def land_start(src, dst, ss, rs):
        @pl.when(home)
        def _():
            pltpu.make_async_copy(src, dst.at[zl], rs.at[zl]).start()

        @pl.when(jnp.logical_not(home))
        def _():
            rc(src, dst.at[zl], ss.at[0], rs.at[zl], swap).start()

        rc(src, dst.at[zl], ss.at[1], rs.at[zl], swap_pair).start()

    def land_wait(src, dst, ss, rs):
        for j in range(2):
            wait(dst.at[j], rs.at[j])

    def land_sent(src, ss):
        @pl.when(jnp.logical_not(home))
        def _():
            wait(src, ss.at[0])

        wait(src, ss.at[1])

    def back_start(src, dst, ss, rs):
        @pl.when(home)
        def _():
            pltpu.make_async_copy(src, dst, rs).start()

        @pl.when(jnp.logical_not(home))
        def _():
            rc(src, dst, ss, rs, swap).start()

    def back_wait(src, dst, ss, rs):
        wait(dst, rs)

        @pl.when(jnp.logical_not(home))
        def _():
            wait(src, ss)

    def small_round(k):
        cp = rc(small, smrecv.at[k], sms.at[k], smr.at[k], (sib, xn, yn, zp, far)[k])
        cp.start()
        cp.wait()
        small[...] = (small[...].astype(F32) + smrecv[k].astype(F32)).astype(BF16)

    def sg_round(k):
        cp = rc(sg, sgrecv.at[k], sgs.at[k], sgr.at[k], (sib, xn, yn, zp, far)[k])
        cp.start()
        cp.wait()
        sg[...] = sg[...] + sgrecv[k]

    half_at = aligned(c * half, half)
    other_at = aligned((1 - c) * half, half)

    def share_start(ref, k, qi):
        part = ref.at[pl.ds(half_at + qi * slot, slot)]
        rc(part, part, cs.at[k, qi], cr.at[k, qi], sib).start()

    def share_wait(ref, k):
        for qi in range(2):
            part = ref.at[pl.ds(other_at + qi * slot, slot)]
            wait(part, cr.at[k, qi])
            wait(part, cs.at[k, qi])

    def sum_start(k, lhs, cols, u, wcols):
        par = k % 2

        def part(at, qi, then):
            rows = pl.ds(at + qi * slot, slot)

            def step(n):
                wrows = pl.ds(aligned(n * NT, NT), NT)
                then(n, dot_nt(lhs[rows, cols], W[u, wrows, wcols]))

            loop(wn, step)

        for qi in range(2):
            lrows = pl.ds(qi * slot, slot)

            def keep(n, v):
                sendA[lrows, pl.ds(aligned(n * NT, NT), NT)] = v.astype(BF16)

            part(other_at, qi, keep)
            rc(sendA.at[lrows], recvA.at[par, lrows], as_.at[k, qi], ar.at[k, qi], sib).start()
        for qi in range(2):
            lrows = pl.ds(qi * slot, slot)
            wait(recvA.at[par, lrows], ar.at[k, qi])

            def add(n, v):
                ncols = pl.ds(aligned(n * NT, NT), NT)
                sendB[lrows, ncols] = (v + recvA[par, lrows, ncols].astype(F32)).astype(BF16)

            part(half_at, qi, add)
            rc(sendB.at[lrows], recvB.at[par, lrows], bs.at[k, qi], br.at[k, qi], zp).start()

    def sum_wait(k, qi):
        wait(recvB.at[k % 2, pl.ds(qi * slot, slot)], br.at[k, qi])

    def sum_sent(k):
        for qi in range(2):
            lrows = pl.ds(qi * slot, slot)
            wait(sendA.at[lrows], as_.at[k, qi])
            wait(sendB.at[lrows], bs.at[k, qi])

    def total(k, rows):
        return sendB[rows, :].astype(F32) + recvB[k % 2, rows, :].astype(F32)

    def tiles(qi, body):
        def step(i):
            body(aligned(qi * slot + i * TILE, TILE))

        loop(slot // TILE, step)

    def norm_tile(v, at, l, which, n_ref, r_ref, a_ref):
        gain = smf[pl.ds(16 * l + 2 * which, 1), :]
        shift = smf[pl.ds(16 * l + 2 * which + 1, 1), :]
        centre = v - jnp.mean(v, axis=1, keepdims=True)
        r = lax.rsqrt(jnp.mean(centre * centre, axis=1, keepdims=True) + EPS)
        n = centre * r
        rows = pl.ds(at, TILE)
        n_ref[l, rows, :] = n.astype(BF16)
        r_ref[l, rows, :] = r
        a_ref[l, pl.ds(aligned(half_at + at, TILE), TILE), :] = (n * gain + shift).astype(BF16)

    def key_valid():
        at = lax.broadcasted_iota(jnp.int32, (1, rows_all), 1)
        quarter = jnp.zeros_like(at)
        for k in range(1, 4):
            quarter = quarter + (at >= k * slot).astype(jnp.int32)
        within = at - quarter * slot
        return jnp.logical_and(within < rows_real, quarter * rows_real + within < VALID)

    lane = lax.broadcasted_iota(jnp.int32, (1, hq), 1)
    QC = 128

    def head_mask(h):
        return jnp.logical_and(lane >= h * HD, lane < (h + 1) * HD)

    qcols = slice(0, hq)
    kcols = slice(hq, 2 * hq)
    vcols = slice(2 * hq, 3 * hq)
    qkvcols = slice(0, 3 * hq)
    ocols = slice(3 * hq, 4 * hq)
    every = slice(0, fq)

    def softmax_of(qm, keys, ok):
        s = jnp.where(ok, dot_nt(qm, keys), FAR_BELOW)
        e = jnp.exp(s - jnp.max(s, axis=1, keepdims=True))
        return e * (1.0 / jnp.sum(e, axis=1, keepdims=True))

    def attention(l):
        def step(i):
            rows = pl.ds(aligned(i * QC, QC), QC)
            qc = qkv[l, rows, qcols].astype(F32)
            keys, values = qkv[l, :, kcols], qkv[l, :, vcols]
            ok = key_valid()
            mixed = jnp.zeros((QC, hq), F32)
            for h in range(heads):
                m = head_mask(h)
                qm = jnp.where(m, qc * (HD ** -0.5), 0.0).astype(BF16)
                p = softmax_of(qm, keys, ok).astype(BF16)
                mixed = jnp.where(m, dot_nn(p, values), mixed)
            o[l, rows, :] = mixed.astype(BF16)

        loop(rows_all // QC, step)

    def attention_back(l):
        dk_acc[...] = jnp.zeros_like(dk_acc)
        dv_acc[...] = jnp.zeros_like(dv_acc)

        def step(i):
            rows = pl.ds(aligned(i * QC, QC), QC)
            qc = qkv[l, rows, qcols].astype(F32)
            oc = ob[rows, :].astype(F32)
            keys, values = qkv[l, :, kcols], qkv[l, :, vcols]
            ok = key_valid()
            dq = jnp.zeros((QC, hq), F32)
            ps, dss, qms, oms = [], [], [], []
            for h in range(heads):
                m = head_mask(h)
                qm = jnp.where(m, qc * (HD ** -0.5), 0.0).astype(BF16)
                om = jnp.where(m, oc, 0.0).astype(BF16)
                p = softmax_of(qm, keys, ok)
                dprob = dot_nt(om, values)
                inner = jnp.sum(dprob * p, axis=1, keepdims=True)
                ds = (p * (dprob - inner)).astype(BF16)
                dq = jnp.where(m, dot_nn(ds, keys), dq)
                ps.append(p.astype(BF16))
                dss.append(ds)
                qms.append(qm)
                oms.append(om)
            dqkv[rows, qcols] = (dq * (HD ** -0.5)).astype(BF16)
            dk_acc[...] += dot_tn(jnp.concatenate(dss, 0), jnp.concatenate(qms, 0))
            dv_acc[...] += dot_tn(jnp.concatenate(ps, 0), jnp.concatenate(oms, 0))

        loop(rows_all // QC, step)
        dqkv[:, kcols] = dk_acc[...].astype(BF16)
        dqkv[:, vcols] = dv_acc[...].astype(BF16)

    def rs1(u):
        ref = W.at[u, pl.ds(diag_blk, kb)]
        rc(ref, recv1.at[u, 0], g1s.at[u, 0], g1r.at[u, 0], xn).start()
        ref = W.at[u, pl.ds(diag_blk + kb, kb)]
        rc(ref, recv1.at[u, 1], g1s.at[u, 1], g1r.at[u, 1], yn).start()

    RT = 64

    def add_rows(u, at, refs, n):
        def step(i):
            off = aligned(i * RT, RT)
            rows = pl.ds(aligned(at + off, RT), RT)
            v = W[u, rows, :].astype(F32)
            for ref in refs:
                v = v + ref[pl.ds(off, RT), :].astype(F32)
            W[u, rows, :] = v.astype(BF16)

        loop(n // RT, step)

    def rs2(u):
        for j in range(2):
            wait(recv1.at[u, j], g1r.at[u, j])
            wait(recv1.at[u, j], g1s.at[u, j])
        add_rows(u, y_blk, [recv1.at[u, 0]], kb)
        ref = W.at[u, pl.ds(y_blk, blk)]
        rc(ref, recv2.at[u, 1], g2s.at[u, 1], g2r.at[u, 1], yn).start()
        add_rows(u, x_blk + kb, [recv1.at[u, 1]], kb)
        ref = W.at[u, pl.ds(x_blk, blk)]
        rc(ref, recv2.at[u, 0], g2s.at[u, 0], g2r.at[u, 0], xn).start()

    def rs3(u):
        for j in range(2):
            wait(recv2.at[u, j], g2r.at[u, j])
            wait(recv2.at[u, j], g2s.at[u, j])
        add_rows(u, own_blk, [recv2.at[u, 0], recv2.at[u, 1]], blk)

        @pl.when(home)
        def _():
            ref = W.at[u, pl.ds(aligned(own_blk + (1 - c) * kb, kb), kb)]
            rc(ref, recv4.at[u, 0], g4s.at[u, 0], g4r.at[u, 0], sib).start()
            ref = W.at[u, pl.ds(aligned(own_blk + c * kb, kb), kb)]
            pltpu.make_async_copy(ref, recv4.at[u, 0], g4r.at[u, 0]).start()

        @pl.when(jnp.logical_not(home))
        def _():
            for j in range(2):
                ref = W.at[u, pl.ds(own_blk + j * kb, kb)]
                rc(ref, recv4.at[u, 1], g4s.at[u, j], g4r.at[u, 1], dev(y, x, j, z2)).start()

    def rs4(u):
        for j in range(2):
            wait(recv4.at[u, j], g4r.at[u, j])
        wait(recv4.at[u, 0], g4s.at[u, 0])

        @pl.when(jnp.logical_not(home))
        def _():
            wait(recv4.at[u, 0], g4s.at[u, 1])

        def step(i):
            rows = pl.ds(aligned(i * RT, RT), RT)
            gw_ref[u, rows, :] = recv4[u, 0, rows, :].astype(F32) + recv4[u, 1, rows, :].astype(F32)

        loop(kb // RT, step)

    def project(l):
        def step(i):
            rows = pl.ds(aligned(i * half, half), half)
            for j in range(3):
                cols = slice(j * hq, (j + 1) * hq)
                v = dot_nn(a1[l, rows, :], W[3 * l, :, cols])
                qkv[l, rows, cols] = (v + qb[8 * l + j:8 * l + j + 1, :]).astype(BF16)

        loop(2, step)

    def expand(l):
        bias_row = pl.ds(16 * l + 8 + q, 1)

        def step(j):
            cols = pl.ds(aligned(j * NT, NT), NT)
            bias = smf[bias_row, cols]

            for i in range(2):
                rows = slice(i * half, (i + 1) * half)
                u = dot_nn(a2[l, rows, :], W[3 * l + 1, :, cols]) + bias
                phi = 0.5 * (1.0 + lax.erf(u * ROOT_HALF))
                act[l, rows, cols] = (u * phi).astype(BF16)
                density = INV_ROOT_2PI * jnp.exp(-0.5 * u * u)
                dgl[l, rows, cols] = (phi + u * density).astype(BF16)

        loop(fq // NT, step)

    def expand_back(l):
        bias_row = pl.ds(16 * l + 8 + q, 1)

        def step(j):
            cols = pl.ds(aligned(j * NT, NT), NT)
            sums = jnp.zeros((1, NT), F32)
            for i in range(2):
                rows = slice(i * half, (i + 1) * half)
                v = dot_nn(gb[rows, :], W[3 * l + 2, :, cols]) * dgl[l, rows, cols].astype(F32)
                low = v.astype(BF16)
                ub[rows, cols] = low
                sums = sums + jnp.sum(low.astype(F32), axis=0, keepdims=True)
            sg[bias_row, cols] = sums

        loop(fq // NT, step)

    def weight_grad(u, lhs, rhs, cols):
        def step(t):
            rows = pl.ds(aligned(t * NT, NT), NT)
            W[u, rows, cols] = dot_tn(lhs[:, rows], rhs[...]).astype(BF16)

        loop(wn, step)

    def acc_add(j, v):
        acc[j] += jnp.sum(v.reshape(TILE // 8, 8, width), axis=0)

    once = (zl == 0).astype(F32)

    def acc_out(j, row):
        sg[row:row + 1, :] = jnp.sum(acc[j], axis=0, keepdims=True) * once

    def norm_back(k, l, which, n_ref, r_ref, low_ref, low_k):
        acc[...] = jnp.zeros_like(acc)
        for qi in range(2):
            sum_wait(k, qi)

            def body(at):
                rows = pl.ds(at, TILE)
                da = total(k, rows)
                n = n_ref[l, rows, :].astype(F32)
                e = da * smf[pl.ds(16 * l + 2 * which, 1), :]
                inner = jnp.mean(e * n, axis=1, keepdims=True)
                middle = jnp.mean(e, axis=1, keepdims=True)
                g = gs[rows, :] + r_ref[l, rows, :] * (e - middle - n * inner)
                gs[rows, :] = g
                acc_add(0, da * n)
                acc_add(1, da)
                acc_add(2, g)
                if low_ref is not None:
                    low_ref[pl.ds(aligned(half_at + at, TILE), TILE), :] = g.astype(BF16)

            tiles(qi, body)
            if low_ref is not None:
                share_start(low_ref, low_k, qi)
        sum_sent(k)
        acc_out(0, 16 * l + 2 * which)
        acc_out(1, 16 * l + 2 * which + 1)
        if which == 1:
            acc_out(2, 16 * l + 4)
        elif l > 0:
            acc_out(2, 16 * (l - 1) + 5)

    s0_start(0)
    land_start(tok, tokst, tks, tkr)
    small[...] = small_in[...]
    small_round(0)
    s0_wait(0)
    s1_start(0)
    s0_start(1)
    s0_start(2)
    land_start(cot, cotst, cts, ctr)
    for k in range(1, 5):
        small_round(k)
    smf[...] = small[...].astype(F32)
    sg[...] = jnp.zeros_like(sg)
    qb[...] = jnp.zeros_like(qb)
    mine = pl.ds(aligned(q * hq, hq), hq)
    for l in range(layers):
        for j, row in ((0, 6), (2, 7)):
            qb[8 * l + j:8 * l + j + 1, :] = smf[16 * l + row:16 * l + row + 1, mine]

    land_wait(tok, tokst, tks, tkr)
    for qi in range(2):
        def first(at, qi=qi):
            v = tokst[qi, pl.ds(aligned(at - qi * slot, TILE), TILE), :].astype(F32)
            xs[pl.ds(at, TILE), :] = v
            norm_tile(v, at, 0, 0, n1, r1, a1)

        tiles(qi, first)
        share_start(a1.at[0], 0, qi)
    pump(0)

    def stream_step(k, l_bias, row, l, which, n_ref, r_ref, a_ref, share_k):
        for qi in range(2):
            sum_wait(k, qi)

            def body(at):
                rows = pl.ds(at, TILE)
                v = xs[rows, :] + total(k, rows) + smf[pl.ds(16 * l_bias + row, 1), :]
                xs[rows, :] = v
                norm_tile(v, at, l, which, n_ref, r_ref, a_ref)

            tiles(qi, body)
            share_start(a_ref.at[l], share_k, qi)
        sum_sent(k)

    for l in range(layers):
        s2_wait(3 * l)
        share_wait(a1.at[l], 2 * l)
        project(l)
        attention(l)
        pump(3 * l + 1)
        sum_start(2 * l, o.at[l], slice(0, hq), 3 * l, ocols)
        if l == 0:
            land_wait(cot, cotst, cts, ctr)
            acc[...] = jnp.zeros_like(acc)
            for qi in range(2):
                def first_back(at, qi=qi):
                    low = cotst[qi, pl.ds(aligned(at - qi * slot, TILE), TILE), :]
                    gs[pl.ds(at, TILE), :] = low.astype(F32)
                    gb[pl.ds(aligned(half_at + at, TILE), TILE), :] = low
                    acc_add(2, low.astype(F32))

                tiles(qi, first_back)
                share_start(gb, 2 * layers, qi)
            acc_out(2, 16 * (layers - 1) + 5)
        stream_step(2 * l, l, 4, l, 1, n2, r2, a2, 2 * l + 1)
        pump(3 * l + 2)
        s2_wait(3 * l + 1)
        share_wait(a2.at[l], 2 * l + 1)
        expand(l)
        s2_wait(3 * l + 2)
        sum_start(2 * l + 1, act.at[l], every, 3 * l + 2, every)
        if l + 1 < layers:
            pump(3 * l + 3)
            stream_step(2 * l + 1, l, 5, l + 1, 0, n1, r1, a1, 2 * l + 2)

    share_wait(gb, 2 * layers)
    k_sum = 2 * layers
    k_share = 2 * layers + 1
    for l in reversed(range(layers)):
        top = l == layers - 1
        if not top:
            share_wait(gb, k_share - 1)
        expand_back(l)
        if top:
            last = k_sum - 1
            for qi in range(2):
                sum_wait(last, qi)

            def finish(i):
                at = aligned(zl * slot + i * TILE, TILE)
                rows = pl.ds(at, TILE)
                v = xs[rows, :] + total(last, rows) + smf[pl.ds(16 * l + 5, 1), :]
                igst[pl.ds(aligned(i * TILE, TILE), TILE), :] = v.astype(BF16)

            loop(slot // TILE, finish)
            sum_sent(last)
            back_start(igst, out_ref, oss.at[0], osr.at[0])
        sum_start(k_sum, ub, every, 3 * l + 1, every)
        for u in (3 * l + 2, 3 * l + 1):
            sends_done(u)
        weight_grad(3 * l + 2, gb, act.at[l], every)
        rs1(3 * l + 2)
        weight_grad(3 * l + 1, a2.at[l], ub, every)
        rs1(3 * l + 1)
        if not top:
            rs3(3 * l + 3)
            rs4(3 * l + 4)
        norm_back(k_sum, l, 1, n2, r2, hb, k_share)
        rs2(3 * l + 2)
        share_wait(hb, k_share)

        def mix_back(i):
            rows = pl.ds(aligned(i * half, half), half)
            ob[rows, :] = dot_nn(hb[rows, :], W[3 * l, :, ocols]).astype(BF16)

        loop(2, mix_back)
        rs2(3 * l + 1)
        attention_back(l)
        sum_start(k_sum + 1, dqkv, qkvcols, 3 * l, qkvcols)
        for row, cols in ((6, qcols), (7, vcols)):
            sg[16 * l + row:16 * l + row + 1, mine] = jnp.sum(
                dqkv[:, cols].astype(F32), axis=0, keepdims=True)
        sends_done(3 * l)
        weight_grad(3 * l, a1.at[l], dqkv, qkvcols)
        weight_grad(3 * l, hb, o.at[l], ocols)
        rs1(3 * l)
        rs3(3 * l + 2)
        if top:
            back_wait(igst, out_ref, oss.at[0], osr.at[0])
        else:
            rs4(3 * l + 3)
        if l > 0:
            norm_back(k_sum + 1, l, 0, n1, r1, gb, k_share + 1)
        else:
            norm_back(k_sum + 1, l, 0, n1, r1, None, None)
        rs2(3 * l)
        rs3(3 * l + 1)
        if l > 0:
            rs4(3 * l + 2)
        k_sum += 2
        k_share += 2

    def finish_grad(i):
        at = aligned(zl * slot + i * TILE, TILE)
        igst[pl.ds(aligned(i * TILE, TILE), TILE), :] = gs[pl.ds(at, TILE), :].astype(BF16)

    loop(slot // TILE, finish_grad)
    back_start(igst, igrecv, oss.at[1], osr.at[1])
    for k in range(3):
        sg_round(k)
    rs3(0)
    for k in range(3, 5):
        sg_round(k)
    rs4(2)
    rs4(1)
    back_wait(igst, igrecv, oss.at[1], osr.at[1])
    ig_ref[...] = igrecv[...].astype(F32)
    rs4(0)
    land_sent(tok, tks)
    land_sent(cot, cts)


def shards(tokens, cotangent, image_mask, qkv_weight, out_weight, up_weight, down_weight,
           qv_bias, up_bias, out_bias, down_bias, attn_gain, attn_shift, mlp_gain, mlp_shift):
    images_here, rows_real, width = tokens.shape
    layers = qkv_weight.shape[0]
    hq = qkv_weight.shape[3]
    fq = up_weight.shape[2]
    lanes = lax.axis_size("tensor")
    groups = lax.axis_size("dp") // 8
    assert images_here == 1 and lanes == 4 and width == fq == 4 * hq
    kb = width // 8
    slot = -(-rows_real // TILE) * TILE
    half = 2 * slot
    rows_all = 4 * slot
    units = 3 * layers
    dp = lax.axis_index("dp")
    z = lax.axis_index("tensor")
    d8 = dp % 8
    first = d8 == 0

    position = z * rows_real + jnp.arange(rows_real)
    keep = (position < VALID).astype(BF16)[:, None] * image_mask.astype(BF16)[0]
    pad = ((0, slot - rows_real), (0, 0))
    tok = jnp.pad(tokens[0], pad)
    cot = jnp.pad(cotangent[0] * keep, pad)

    here = qkv_weight.shape[1]
    wsh = jnp.stack([
        jnp.concatenate([qkv_weight.reshape(layers, here, 3 * hq), out_weight], axis=2),
        up_weight, down_weight], axis=1).reshape(units, here, fq)
    if groups > 1:
        wsh = lax.all_gather(wsh, "dp", axis=1, tiled=True)
        wsh = lax.dynamic_slice_in_dim(wsh, d8 * kb, kb, 1)

    shard = dp * lanes + z
    piece = attn_gain.shape[1]

    def window(values, at):
        wide = jnp.zeros((values.shape[0], width), BF16)
        return lax.dynamic_update_slice(wide, values, (0, at))

    ups = up_bias.shape[1]
    up_at = shard * ups
    rows = []
    for l in range(layers):
        six = jnp.stack([attn_gain[l], attn_shift[l], mlp_gain[l], mlp_shift[l],
                         out_bias[l], down_bias[l], qv_bias[l, 0], qv_bias[l, 1]])
        rows.append(window(six, shard * piece))
        up_row = window(up_bias[l][None], up_at % width)
        rows.append(jnp.where(jnp.arange(4)[:, None] == up_at // width, up_row, 0))
        rows.append(jnp.zeros((4, width), BF16))
    small_in = jnp.concatenate(rows)
    if groups > 1:
        small_in = lax.psum(small_in, "dp") * first.astype(BF16)

    out_shapes = (
        jax.ShapeDtypeStruct((slot, width), BF16),
        jax.ShapeDtypeStruct((slot, width), F32),
        jax.ShapeDtypeStruct((units, kb, fq), F32),
        jax.ShapeDtypeStruct((16 * layers, width), F32),
    )
    V = pltpu.VMEM
    D = lambda *s: pltpu.SemaphoreType.DMA(s)
    sums, shares = 4 * layers, 4 * layers
    scratch = [
        V((units, width, fq), BF16),
        V((half, width), F32), V((half, width), F32),
        V((layers, half, width), BF16), V((layers, half, width), BF16),
        V((layers, half, 1), F32), V((layers, half, 1), F32),
        V((layers, rows_all, width), BF16), V((layers, rows_all, width), BF16),
        V((layers, rows_all, 3 * hq), BF16), V((layers, rows_all, hq), BF16),
        V((layers, rows_all, fq), BF16), V((layers, rows_all, fq), BF16),
        V((rows_all, width), BF16), V((rows_all, width), BF16),
        V((rows_all, fq), BF16), V((rows_all, hq), BF16), V((rows_all, 3 * hq), BF16),
        V((rows_all, hq), F32), V((rows_all, hq), F32), V((3, 8, width), F32),
        V((half, width), BF16), V((2, half, width), BF16),
        V((half, width), BF16), V((2, half, width), BF16),
        V((2, slot, width), BF16), V((2, slot, width), BF16),
        V((slot, width), BF16), V((slot, width), BF16),
        V((16 * layers, width), BF16), V((5, 16 * layers, width), BF16),
        V((16 * layers, width), F32), V((8 * layers, hq), F32),
        V((5, 16 * layers, width), F32),
        V((units, 2, kb, fq), BF16), V((units, 2, 2 * kb, fq), BF16), V((units, 2, kb, fq), BF16),
        D(units, 2), D(units, 2), D(units, 2), D(units, 2), D(units, 2), D(units, 2),
        D(sums, 2), D(sums, 2), D(sums, 2), D(sums, 2), D(shares, 2), D(shares, 2),
        D(2), D(2), D(2), D(2), D(2), D(2), D(5), D(5), D(5), D(5),
        D(units, 2), D(units, 2), D(units, 2), D(units, 2), D(units, 2), D(units, 2),
    ]
    any_spec = pl.BlockSpec(memory_space=pl.ANY)
    vmem_spec = pl.BlockSpec(memory_space=pltpu.VMEM)
    out, ig, gw, sg = pl.pallas_call(
        functools.partial(kernel, layers, rows_real),
        out_shape=out_shapes,
        in_specs=[any_spec, any_spec, any_spec, vmem_spec],
        out_specs=(any_spec, vmem_spec, vmem_spec, vmem_spec),
        scratch_shapes=scratch,
        compiler_params=pltpu.CompilerParams(
            collective_id=0, has_side_effects=True, vmem_limit_bytes=63 * 2 ** 20),
        cost_estimate=pl.CostEstimate(
            flops=int(1e11), bytes_accessed=int(1e8), transcendentals=0),
    )(tok, cot, wsh, small_in)

    if groups > 1:
        wide = lax.dynamic_update_slice_in_dim(
            jnp.zeros((units, width, fq), F32), gw, d8 * kb, 1)
        gw = lax.psum_scatter(wide, "dp", scatter_dimension=1, tiled=True)
        sg = lax.psum(sg * first.astype(F32), "dp")
    gw = gw.reshape(layers, 3, here, fq)
    sg = sg.reshape(layers, 16, width)
    mine = lax.dynamic_slice_in_dim(sg[:, :8], shard * piece, piece, 2)
    ups_grad = lax.dynamic_slice_in_dim(sg[:, 8:12].reshape(layers, 4 * width), up_at, ups, 1)
    return (
        out[:rows_real][None],
        ig[:rows_real][None],
        gw[:, 0, :, :3 * hq].reshape(layers, here, 3, hq),
        gw[:, 0, :, 3 * hq:],
        gw[:, 1],
        gw[:, 2],
        mine[:, 6:8],
        ups_grad,
        mine[:, 4],
        mine[:, 5],
        mine[:, 0],
        mine[:, 1],
        mine[:, 2],
        mine[:, 3],
    )


def solution(mesh):
    both = ("dp", "tensor")
    rows = P("dp", "tensor", None)
    cols = P(None, "dp", "tensor")
    vec = P(None, both)
    return jax.shard_map(
        shards,
        mesh=mesh,
        in_specs=(rows, rows, P("dp"), P(None, "dp", None, "tensor"), cols, cols, cols,
                  P(None, None, both), vec, vec, vec, vec, vec, vec, vec),
        out_specs=(rows, rows, P(None, "dp", None, "tensor"), cols, cols, cols,
                   P(None, None, both), vec, vec, vec, vec, vec, vec, vec),
        check_vma=False,
    )
```

time: 2700 us -> 411 us (0.15)
  waiting for transfers between devices: 1630 us -> 0 us
  blocking collectives: 759 us -> 0 us
  Pallas kernels: 0 us -> 384 us
  matrix products: 122 us -> 0 us
  other arithmetic: 72.5 us -> 1.36 us
  local copies, waits for them, and re-layouts: 72.8 us -> 23.9 us
    unnamed x46 -> x0, waiting for transfers between devices: 939 us -> none
    all_gather x10 -> x0, blocking collectives: 544 us -> none  [the longest x1 69.5 us: shards(): lax.all_gather(attn_gain, ('dp', 'tensor'), axis=1, tiled=True)]
    reduce_scatter x8 -> x0, waiting for transfers between devices: 387 us -> none  [the longest x2 108 us: shards(): lax.psum_scatter(down_grad, 'dp', scatter_dimension=0, tiled=True)]
    pallas_call x0 -> x1, Pallas kernels: none -> 384 us  [shards(): pl.pallas_call(functools.partial(kernel, layers, rows_real), out_shape=ou...]
    all_gather x14 -> x0, waiting for transfers between devices: 304 us -> none  [the longest x4 194 us: gather_grads(): return lax.all_gather(grad_low, 'tensor', axis=1, tiled=True)]
    unnamed x7 -> x0, blocking collectives: 215 us -> none
    dot_general x36 -> x0, matrix products: 122 us -> none  [the longest x2 11.9 us: shards(): jnp.einsum('isd,isf->df', grad_rows_one, activated, preferred_element_typ...]
    unnamed x197 -> x21, local copies, waits for them, and re-layouts: 54.5 us -> 6 us
  transfers between devices with their start and end apart: 38 -> 0, of which waited for: 28 -> 0; matrix products, arithmetic and copies ran while one was open for 11% -> 0% of each run, Pallas kernels for 0% -> 0%
where the time goes in v1:
time: 411 us
  Pallas kernels  384 us (93%)
  local copies, waits for them, and re-layouts  23.9 us (6%)
    pallas_call x1, Pallas kernels, shards(): pl.pallas_call(functools.partial(kernel, layers, rows_real), out_shape=ou...  384 us

profile of v1, /device:TPU:0, one launch (start us, length us, event | category | flops | bytes accessed | tf_op | source)
XLA Modules:
  0.0 411.0 jit_solution(5418300115261239413)
XLA Ops:
  0.6 0.0 copy-start.4
  0.7 0.0 copy-start.5
  1.4 0.7 slice_bitcast_fusion.6
  2.2 0.2 dynamic_update_slice.17
  2.4 0.2 dynamic_update_slice.15
  2.6 0.7 slice_bitcast_fusion.7
  3.3 0.7 fusion
  4.1 0.7 fusion.4
  4.8 0.7 fusion.2
  5.6 0.1 broadcast_select_fusion
  5.7 0.2 dynamic_update_slice.14
  5.9 0.2 dynamic_update_slice.16
  6.1 2.5 concatenate.7.small_in
  8.5 1.0 copy.36
  9.6 1.1 bitcast_multiply_fusion
  10.6 0.0 copy-start.2
  10.7 0.8 pad.8.cot
  11.4 0.0 copy-done.5
  11.4 0.8 pad.7.tok
  12.2 0.0 copy-done.4
  12.2 0.0 copy-start.3
  12.2 0.2 copy.35
  12.4 0.0 copy-done.2
  12.4 0.3 copy.37
  12.7 0.5 copy-done.3
  13.2 0.3 copy.38
  13.5 0.2 pad_maximum_fusion
  13.7 1.6 copy.39
  15.2 384.2 %shard_map.254 = (bf16[160,1024]{1,0:T(8,128)(2,1)}, f32[160,1024]{1,0:T(8,128)}, f32[6,128,1024]{2,1,0:T(8,128)}, f32[32,1024]{1,0:T(8,128)}) custom-call(bf16[160,1024]{1,0:T(8,128)(2,1)} %pad.7.tok, bf16[160,1024]{1,0:T(8,128)(2,1)} %pad.8.cot, bf16[6,128,1024]{2,1,0:T(8,128)(2,1)} %bitcast.56, bf16[32,1024]{1,0:T(8,128)(2,1)} %concatenate.7.small_in), custom_call_target="tpu_custom_call" | custom-call | flops 99999997952 | bytes 100000000 | tf_op jit(solution)/shard_map/pallas_call | solution.py:778
  399.4 0.0 copy-start.1
  399.4 1.8 slice_bitcast_fusion.3
  401.2 0.8 slice_bitcast_fusion.5
  402.0 0.0 copy-start
  402.0 1.0 slice.136
  403.1 0.6 constant_dynamic-slice_fusion.6
  403.6 0.7 constant_dynamic-slice_fusion.5
  404.3 0.7 constant_dynamic-slice_fusion.7
  404.9 1.7 slice_bitcast_fusion.4
  406.6 0.0 copy-done.1
  406.7 1.4 copy.44
  408.1 0.0 copy-done
  408.1 0.1 slice.132
  408.2 1.5 slice_bitcast_fusion
  409.6 0.3 copy.46
  409.9 1.2 copy.45
  (12 shorter events, 0.2 us)
Async XLA Ops:
  0.6 11.5 %copy-start.4 = (bf16[2,128,3,256]{3,1,2,0:T(8,128)(2,1)S(1)}, bf16[2,128,3,256]{3,1,2,0:T(8,128)(2,1)}, u32[]{:S(2)}) copy-start(bf16[2,128,3,256]{3,1,2,0:T(8,128)(2,1)} %param.18) | copy-start | bytes 1179652
  0.7 10.8 %copy-start.5 = (bf16[1,146,1024]{2,1,0:T(8,128)(2,1)S(1)}, bf16[1,146,1024]{2,1,0:T(8,128)(2,1)}, u32[]{:S(2)}) copy-start(bf16[1,146,1024]{2,1,0:T(8,128)(2,1)} %param.15) | copy-start | bytes 897028
  10.6 1.8 copy-start.2
  12.2 1.0 copy-start.3
  399.4 7.2 %copy-start.1 = (f32[160,1024]{1,0:T(8,128)S(1)}, f32[160,1024]{1,0:T(8,128)}, u32[]{:S(2)}) copy-start(f32[160,1024]{1,0:T(8,128)} %get-tuple-element.19) | copy-start | bytes 1966084
  402.0 6.1 %copy-start = (f32[6,128,1024]{2,1,0:T(8,128)S(1)}, f32[6,128,1024]{2,1,0:T(8,128)}, u32[]{:S(2)}) copy-start(f32[6,128,1024]{2,1,0:T(8,128)} %get-tuple-element.20) | copy-start | bytes 9437188
